TPU v7x, 32 devices: a whole 2x2x4 slice. The times are simulated.
32 devices in a mesh: tank: 2 (over y), slab: 4 (over z), cross: 2 (over x), sub: 2 (over core).
Axes of the slice: x: 2, y: 2, z: 4, core: 2. Of those that a mesh axis runs over, the one named last changes fastest.
Arguments:
- positions: float32 [3, 64, 64, 128], P(None, ('tank', 'slab'), ('cross', 'sub')), parts along dimension 1, as said below
- velocities: float32 [3, 64, 64, 128], P(None, ('tank', 'slab'), ('cross', 'sub')), parts along dimension 1, may hold values from -6 to 6
- pair_i: int32 [8, 4, 1152], P(('tank', 'slab'), ('cross', 'sub')), parts along dimension 0, may hold values from 0 to 127, as said below
- pair_j: int32 [8, 4, 1152], P(('tank', 'slab'), ('cross', 'sub')), parts along dimension 0, may hold values from 0 to 179, as said below
- pair_count: int32 [8, 4], P(('tank', 'slab'), ('cross', 'sub')), parts along dimension 0, may hold values from 128 to 1152, as said below
- block_fill: int32 [64, 64], P(('tank', 'slab'), ('cross', 'sub')), parts along dimension 0, may hold values from 0 to 128, as said below
- block_body: int32 [64, 64], P(('tank', 'slab'), ('cross', 'sub')), parts along dimension 0, may hold values from 0 to 4
Outputs:
- density: float32 [64, 64, 128], P(('tank', 'slab'), ('cross', 'sub')), parts along dimension 0
- accel: float32 [3, 64, 64, 128], P(None, ('tank', 'slab'), ('cross', 'sub')), parts along dimension 1
- body_force: float32 [3, 8], P(None, 'tank'), parts along dimension 1
There are 2 independent parts, one for each index of `tank`. A program takes and returns all parts, laid end to end along the dimension named above; each array names one. Nothing has to cross between parts.
Inputs may be any that keep to these rules, and one draw needn't show every extreme that they name: `pair_i`: slots 0 to 127 of each row pair local block k with itself (extended block (k // 16 + 1) (18) + k % 16 + 1); the other slots pair each local block once with each of its eight neighbouring extended blocks, in a drawn order, those in which both blocks lie in the tank and have block_fill above 0 coming first. `pair_j`: see pair_i. pair_count is 128 plus the number of neighbour slots whose two blocks both lie in the tank and have block_fill above 0. `block_fill`: a block holds either no particles or 64 to 128. `block_body`: the value 4 marks a free fluid block. `positions`: particles of global block (a, b) have first coordinate in [2.6 a, 2.6 (a + 1)), second in [2.6 b, 2.6 (b + 1)) and third in [0, 18.9).
All inputs are finite; a program needn't handle non-finite values.
Results may differ from a plain program's by a relative error of at most 0.0003.
Values sent between devices are 32-bit elements; how exact they have to be, the bound alone decides.
A program may use at most 64 MiB of HBM per device.

v0:
```python
import math
import jax
import jax.numpy as jnp
from jax import lax
from jax.sharding import PartitionSpec as P

NBODY = 4
SMOOTH = 1.3
KERNEL_NORM = 21.0 / (16.0 * math.pi * SMOOTH**3)
SLOPE_NORM = 5.0 * KERNEL_NORM / SMOOTH**2
VISCOSITY = 0.2
GRAVITY = 1.0


def padded(shard, sides, width):
    for axis, dim in sides:
        devices, length = (lax.axis_size(axis), shard.shape[dim])
        up = [(i, (i + 1) % devices) for i in range(devices - 1)]
        down = [(j, i) for i, j in up]
        last = lax.slice_in_dim(shard, length - width, length, axis=dim)
        initial = lax.slice_in_dim(shard, 0, width, axis=dim)
        before = lax.ppermute(last, axis, up)
        after = lax.ppermute(initial, axis, down)
        shard = jnp.concatenate([before, shard, after], axis=dim)
    return shard


def pair_shape(first_tiles, second_tiles):
    offsets = first_tiles[:, 0:3, :, None] - second_tiles[:, 0:3, None, :]
    distance = jnp.sqrt(jnp.sum(offsets * offsets, axis=1)) / SMOOTH
    remain = jnp.maximum(1.0 - 0.5 * distance, 0.0)
    return (offsets, distance, remain)


def density_terms(first_tiles, second_tiles):
    offsets, distance, remain = pair_shape(first_tiles, second_tiles)
    kernel = KERNEL_NORM * remain**4 * (2.0 * distance + 1.0)
    return jnp.sum(kernel * second_tiles[:, 3, None, :], axis=2)


def force_terms(first_tiles, second_tiles):
    offsets, distance, remain = pair_shape(first_tiles, second_tiles)
    slope = SLOPE_NORM * remain**3 * second_tiles[:, 3, None, :]
    pushed = slope * (first_tiles[:, 7, :, None] + second_tiles[:, 7, None, :])
    push_sum = jnp.sum(pushed[:, None] * offsets, axis=3)
    drift = first_tiles[:, 4:7, :, None] - second_tiles[:, 4:7, None, :]
    drag_sum = jnp.sum(slope[:, None] * drift, axis=3)
    return push_sum - VISCOSITY * drag_sum


def tile_loop(
    begin_slot, end_slot, total_slots, group_size, fetch_tiles, kernel, store_values, initial
):
    first_group = begin_slot // group_size
    last_group = (end_slot + group_size - 1) // group_size

    def advance(group_index, carried):
        nominal = group_index * group_size
        anchor = jnp.minimum(nominal, total_slots - group_size).astype(jnp.int32)
        slot_ids = anchor + lax.broadcasted_iota(jnp.int32, (group_size,), 0)
        wanted = (slot_ids >= jnp.maximum(begin_slot, nominal)) & (
            slot_ids < jnp.minimum(end_slot, nominal + group_size)
        )
        first_tiles, second_tiles = fetch_tiles(anchor)
        values = kernel(first_tiles, second_tiles)
        weight = wanted.astype(jnp.float32).reshape((group_size,) + (1,) * (values.ndim - 1))
        return store_values(carried, anchor, values * weight)

    return lax.fori_loop(first_group, last_group, advance, initial)


def table_fetch(table, firsts, seconds, group_size):

    def fetch_tiles(anchor):
        first_ids = lax.dynamic_slice_in_dim(firsts, anchor, group_size)
        second_ids = lax.dynamic_slice_in_dim(seconds, anchor, group_size)
        return (jnp.take(table, first_ids, axis=0), jnp.take(table, second_ids, axis=0))

    return fetch_tiles


def scatter_store(targets, group_size):

    def store_values(carried, anchor, values):
        target_ids = lax.dynamic_slice_in_dim(targets, anchor, group_size)
        return carried.at[target_ids].add(values)

    return store_values


def shards(positions, velocities, pair_i, pair_j, pair_count, block_fill, block_body):
    lengthwise, columns = block_fill.shape
    local_count = lengthwise * columns
    frame_width = columns + 2
    slot_ids = lax.broadcasted_iota(jnp.int32, (lengthwise, columns, 128), 2)
    masses = (slot_ids < block_fill[:, :, None]).astype(jnp.float32)
    state = jnp.concatenate(
        [
            jnp.transpose(positions, (1, 2, 0, 3)),
            masses[:, :, None, :],
            jnp.transpose(velocities, (1, 2, 0, 3)),
        ],
        axis=2,
    )
    framed = padded(state, (("slab", 0), (("cross", "sub"), 1)), 1)
    table = framed.reshape((lengthwise + 2) * frame_width, 7, 128)
    local_firsts = pair_i.reshape(-1)
    ext_firsts = (local_firsts // columns + 1) * frame_width + local_firsts % columns + 1
    ext_seconds = pair_j.reshape(-1)
    total_slots = local_firsts.shape[0]
    live_count = pair_count.reshape(())
    group_size = min(16, 2 * local_count, total_slots)
    density_sums = tile_loop(
        0,
        live_count,
        total_slots,
        group_size,
        table_fetch(table, ext_firsts, ext_seconds, group_size),
        density_terms,
        scatter_store(local_firsts, group_size),
        jnp.zeros((local_count, 128), jnp.float32),
    )
    valid = masses.reshape(local_count, 128)
    density = density_sums * valid
    safe_density = jnp.where(valid > 0, density_sums, 1.0)
    pressure_term = valid * (safe_density**7 - 1.0) / (safe_density * safe_density)
    framed_pressure = padded(
        pressure_term.reshape(lengthwise, columns, 1, 128), (("slab", 0), (("cross", "sub"), 1)), 1
    )
    force_table = jnp.concatenate([table, framed_pressure.reshape(-1, 1, 128)], axis=1)
    hydro_start = jnp.zeros((local_count, 3, 128), jnp.float32)
    hydro = tile_loop(
        0,
        live_count,
        total_slots,
        group_size,
        table_fetch(force_table, ext_firsts, ext_seconds, group_size),
        force_terms,
        scatter_store(local_firsts, group_size),
        hydro_start,
    )
    hydro = hydro * valid[:, None, :]
    nothing = jnp.zeros_like(valid)
    gravity = jnp.stack([nothing, nothing, GRAVITY * valid], axis=1)
    accel = jnp.transpose((hydro - gravity).reshape(lengthwise, columns, 3, 128), (2, 0, 1, 3))
    block_sums = jnp.sum(hydro, axis=2)
    owners = (
        block_body.reshape(local_count)[:, None]
        == lax.broadcasted_iota(jnp.int32, (local_count, NBODY), 1)
    ).astype(jnp.float32)
    partial_force = jnp.dot(block_sums.T, owners, precision=lax.Precision.HIGHEST)
    totals = lax.psum(partial_force, ("slab", "cross", "sub"))
    slot_total = (
        128
        * lengthwise
        * lax.axis_size("slab")
        * columns
        * lax.axis_size("cross")
        * lax.axis_size("sub")
    )
    body_force = totals / math.sqrt(slot_total)
    return (density.reshape(lengthwise, columns, 128), accel, body_force)


def solution(mesh):
    placed = (
        P(None, ("tank", "slab"), ("cross", "sub"), None),
        P(None, ("tank", "slab"), ("cross", "sub"), None),
        P(("tank", "slab"), ("cross", "sub"), None),
        P(("tank", "slab"), ("cross", "sub"), None),
        P(("tank", "slab"), ("cross", "sub")),
        P(("tank", "slab"), ("cross", "sub")),
        P(("tank", "slab"), ("cross", "sub")),
    )
    return jax.shard_map(
        shards,
        mesh=mesh,
        in_specs=placed,
        out_specs=(
            P(("tank", "slab"), ("cross", "sub"), None),
            P(None, ("tank", "slab"), ("cross", "sub"), None),
            P(None, "tank"),
        ),
        check_vma=False,
    )
```

profile of v0, /device:TPU:0, one launch (start us, length us, event | category | flops | bytes accessed | tf_op | source)
XLA Modules:
  0.0 1040.7 jit_solution(2760082690979434666)
XLA Ops:
  2.3 4.9 collective-permute-start
  9.3 4.1 collective-permute-done.1
  17.8 2.7 collective-permute-done.3
  21.0 267.2 %while.24 = (s32[]{:T(128)}, f32[128,128]{1,0:T(8,128)S(1)}, s32[]{:T(128)}, s32[1152]{0:T(1024)S(1)}, s32[1152]{0:T(1024)S(1)}, /*index=5*/f32[180,7,128]{2,1,0...) while((s32[]{:T(128)}, f32[128,128]{1,0:T(8,128)S(1)}, ...), condition=%wide.region_4.6_spmd, body=%wide.region_0.5_spmd.sunk | while | flops 5005642 | bytes 2704879 | solution.py:69
  291.6 77.5 %collective-permute-done.5 = f32[1,16,1,128]{3,1,2,0:T(8,128)S(1)} collective-permute-done((f32[1,16,1,128]{3,1,2,0:T(8,128)S(1)}, f32[1,16,1,128]{3,1,2,0:T(8,128)S(1)}, u32[]{:S(2)}, u32[]{:S(2)}) %collective-permute-start.5) | collective-permute-done | bytes 8224 | tf_op jit(solution)/shard_map/ppermute | solution.py:23
  369.1 8.2 collective-permute-start.6
  378.9 2.1 collective-permute-done.7
  381.3 494.1 %while.25 = (s32[]{:T(128)}, f32[128,3,128]{2,1,0:T(4,128)S(1)}, s32[]{:T(128)}, s32[1152]{0:T(1024)S(1)}, s32[1152]{0:T(1024)S(1)}, /*index=5*/f32[180,8,128]{2...) while((s32[]{:T(128)}, f32[128,3,128]{2,1,0:T(4,128)S(1)}, ...), condition=%wide.region_10.13_spmd, body=%wide.region_5.12_spmd.sunk | while | flops 8962378 | bytes 7439471 | solution.py:69
  384.4 1.9 multiply_reduce_fusion.9
  393.2 1.9 multiply_reduce_fusion.9
  402.1 1.9 multiply_reduce_fusion.9
  410.9 1.9 multiply_reduce_fusion.9
  419.7 1.9 multiply_reduce_fusion.9
  428.5 1.9 multiply_reduce_fusion.9
  437.4 1.9 multiply_reduce_fusion.9
  446.2 1.9 multiply_reduce_fusion.9
  455.0 1.9 multiply_reduce_fusion.9
  463.8 1.9 multiply_reduce_fusion.9
  472.6 1.9 multiply_reduce_fusion.9
  481.5 1.9 multiply_reduce_fusion.9
  490.3 1.9 multiply_reduce_fusion.9
  499.1 1.9 multiply_reduce_fusion.9
  507.9 1.9 multiply_reduce_fusion.9
  516.8 1.9 multiply_reduce_fusion.9
  525.6 1.9 multiply_reduce_fusion.9
  534.4 1.9 multiply_reduce_fusion.9
  587.3 1.9 multiply_reduce_fusion.9
  605.0 1.9 multiply_reduce_fusion.9
  640.3 1.9 multiply_reduce_fusion.9
  737.3 1.9 multiply_reduce_fusion.9
  799.1 1.9 multiply_reduce_fusion.9
  876.6 163.5 %psum.7 = f32[3,4]{1,0:T(4,128)S(1)} all-reduce(f32[3,4]{1,0:T(4,128)S(1)} %fusion.12), channel_id=1, replica_groups=mesh['tank'=2,'slab'=4,'cross'=2,'sub'=2] {'slab','cross','sub'}, use_global_device_ids=true, to_apply=%region_12.15 | all-reduce | flops 12 | bytes 96 | tf_op jit(solution)/shard_map/psum | solution.py:152
  (1868 shorter events, 645.4 us)
Async XLA Ops:
  0.6 17.1 %copy-start.2 = (s32[8,16]{1,0:T(8,128)S(1)}, s32[8,16]{1,0:T(8,128)}, u32[]{:S(2)}) copy-start(s32[8,16]{1,0:T(8,128)} %param.20) | copy-start | bytes 1540
  0.6 19.9 %copy-start.1 = (f32[3,8,16,128]{3,2,1,0:T(8,128)S(1)}, f32[3,8,16,128]{3,2,1,0:T(8,128)}, u32[]{:S(2)}) copy-start(f32[3,8,16,128]{3,2,1,0:T(8,128)} %param.15) | copy-start | bytes 589828
  0.7 19.9 %copy-start = (f32[3,8,16,128]{3,2,1,0:T(8,128)S(1)}, f32[3,8,16,128]{3,2,1,0:T(8,128)}, u32[]{:S(2)}) copy-start(f32[3,8,16,128]{3,2,1,0:T(8,128)} %param.16) | copy-start | bytes 589828
  0.7 17.1 %copy-start.3 = (s32[1,1,1152]{2,1,0:T(1,128)S(1)}, s32[1,1,1152]{2,1,0:T(1,128)}, u32[]{:S(2)}) copy-start(s32[1,1,1152]{2,1,0:T(1,128)} %param.18) | copy-start | bytes 13828
  2.3 7.0 collective-permute-start
  7.3 6.1 collective-permute-start.1
  14.4 3.4 collective-permute-start.2
  15.7 4.8 collective-permute-start.3
  21.0 357.8 %copy-start.4 = (s32[8,16]{1,0:T(8,128)S(1)}, s32[8,16]{1,0:T(8,128)}, u32[]{:S(2)}) copy-start(s32[8,16]{1,0:T(8,128)} %param.21) | copy-start | bytes 1540
  288.9 2.7 collective-permute-start.4
  290.2 78.9 %collective-permute-start.5 = (f32[1,16,1,128]{3,1,2,0:T(8,128)S(1)}, f32[1,16,1,128]{3,1,2,0:T(8,128)S(1)}, u32[]{:S(2)}, u32[]{:S(2)}) collective-permute-start(f32[1,16,1,128]{3,1,2,0:T(8,128)S(1)} %get-tuple-element.279), channel_id=1, source_target_pairs={{4,0},{8,4},{12,8},{5,1},{9,5},{13,9},{6,2},{10,6},{14,10},{7,3},{... | collective-permute-start | bytes 24584 | tf_op jit(solution)/shard_map/ppermute | solution.py:23
  369.1 9.8 collective-permute-start.6
  377.3 3.7 collective-permute-start.7
where the time goes:
time: 1040 us
  other arithmetic  550 us (53%)
  blocking collectives  164 us (16%)
  local copies, waits for them, and re-layouts  131 us (13%)
  loops' own time  87.8 us (8%)
  waiting for transfers between devices  86.4 us (8%)
  starting transfers between devices  20.9 us (2%)
    psum x1, blocking collectives, shards(): totals = lax.psum(partial_force, ('slab', 'cross', 'sub'))  164 us
    reduce_sum x112, other arithmetic, pair_shape(): distance = jnp.sqrt(jnp.sum(offsets * offsets, axis=1)) / SMOOTH  116 us
    reduce_sum x56, other arithmetic, force_terms(): drag_sum = jnp.sum(slope[:, None] * drift, axis=3)  105 us
    reduce_sum x56, other arithmetic, force_terms(): push_sum = jnp.sum(pushed[:, None] * offsets, axis=3)  104 us
    scatter-add x112, other arithmetic, store_values(): return carried.at[target_ids].add(values)  104 us
    another operation x2, loops' own time, tile_loop(): return lax.fori_loop(first_group, last_group, advance, initial)  87.8 us
    ppermute x4, waiting for transfers between devices, padded(): after = lax.ppermute(initial, axis, down)  86.3 us
    gather x112, local copies, waits for them, and re-layouts, fetch_tiles(): jnp.take(table, second_ids, axis=0)  63.3 us
  transfers between devices with their start and end apart: 8, of which 4 were waited for; matrix products, arithmetic and copies ran while one was open for 0% of the time, Pallas kernels for 0%

commit v1 on v0

--- a/solution.py
+++ b/solution.py
@@ -149,7 +149,7 @@
         == lax.broadcasted_iota(jnp.int32, (local_count, NBODY), 1)
     ).astype(jnp.float32)
     partial_force = jnp.dot(block_sums.T, owners, precision=lax.Precision.HIGHEST)
-    totals = lax.psum(partial_force, ("slab", "cross", "sub"))
+    totals = jnp.sum(lax.all_gather(partial_force, ("slab", "cross", "sub")), axis=0)
     slot_total = (
         128
         * lengthwise

time: 1040 us -> 1040 us (level)
    psum x1 -> x0, blocking collectives: 164 us -> none  [shards(): totals = lax.psum(partial_force, ('slab', 'cross', 'sub'))]
    all_gather x0 -> x1, blocking collectives: none -> 160 us  [shards(): lax.all_gather(partial_force, ('slab', 'cross', 'sub'))]
where the time goes in v1:
time: 1040 us
  other arithmetic  550 us (53%)
  blocking collectives  160 us (15%)
  local copies, waits for them, and re-layouts  131 us (13%)
  loops' own time  87.8 us (8%)
  waiting for transfers between devices  86.4 us (8%)
  starting transfers between devices  20.9 us (2%)
    all_gather x1, blocking collectives, shards(): lax.all_gather(partial_force, ('slab', 'cross', 'sub'))  160 us
    reduce_sum x112, other arithmetic, pair_shape(): distance = jnp.sqrt(jnp.sum(offsets * offsets, axis=1)) / SMOOTH  116 us
    reduce_sum x56, other arithmetic, force_terms(): drag_sum = jnp.sum(slope[:, None] * drift, axis=3)  105 us
    reduce_sum x56, other arithmetic, force_terms(): push_sum = jnp.sum(pushed[:, None] * offsets, axis=3)  104 us
    scatter-add x112, other arithmetic, store_values(): return carried.at[target_ids].add(values)  104 us
    another operation x2, loops' own time, tile_loop(): return lax.fori_loop(first_group, last_group, advance, initial)  87.8 us
    ppermute x4, waiting for transfers between devices, padded(): after = lax.ppermute(initial, axis, down)  86.3 us
    gather x112, local copies, waits for them, and re-layouts, fetch_tiles(): jnp.take(table, second_ids, axis=0)  63.3 us
  transfers between devices with their start and end apart: 8, of which 4 were waited for; matrix products, arithmetic and copies ran while one was open for 0% of the time, Pallas kernels for 0%

profile of v1, /device:TPU:0, one launch (start us, length us, event | category | flops | bytes accessed | tf_op | source)
XLA Modules:
  0.0 1036.9 jit_solution(16932009715573856771)
XLA Ops:
  2.3 4.9 collective-permute-start
  9.3 4.1 collective-permute-done.1
  17.8 2.7 collective-permute-done.3
  21.0 267.2 %while.24 = (s32[]{:T(128)}, f32[128,128]{1,0:T(8,128)S(1)}, s32[]{:T(128)}, s32[1152]{0:T(1024)S(1)}, s32[1152]{0:T(1024)S(1)}, /*index=5*/f32[180,7,128]{2,1,0...) while((s32[]{:T(128)}, f32[128,128]{1,0:T(8,128)S(1)}, ...), condition=%wide.region_4.6_spmd, body=%wide.region_0.5_spmd.sunk | while | flops 5005642 | bytes 2704879 | solution.py:69
  291.6 77.5 %collective-permute-done.5 = f32[1,16,1,128]{3,1,2,0:T(8,128)S(1)} collective-permute-done((f32[1,16,1,128]{3,1,2,0:T(8,128)S(1)}, f32[1,16,1,128]{3,1,2,0:T(8,128)S(1)}, u32[]{:S(2)}, u32[]{:S(2)}) %collective-permute-start.5) | collective-permute-done | bytes 8224 | tf_op jit(solution)/shard_map/ppermute | solution.py:23
  369.1 8.2 collective-permute-start.6
  378.9 2.1 collective-permute-done.7
  381.3 494.1 %while.25 = (s32[]{:T(128)}, f32[128,3,128]{2,1,0:T(4,128)S(1)}, s32[]{:T(128)}, s32[1152]{0:T(1024)S(1)}, s32[1152]{0:T(1024)S(1)}, /*index=5*/f32[180,8,128]{2...) while((s32[]{:T(128)}, f32[128,3,128]{2,1,0:T(4,128)S(1)}, ...), condition=%wide.region_10.13_spmd, body=%wide.region_5.12_spmd.sunk | while | flops 8962378 | bytes 7439471 | solution.py:69
  384.4 1.9 multiply_reduce_fusion.9
  393.2 1.9 multiply_reduce_fusion.9
  402.1 1.9 multiply_reduce_fusion.9
  410.9 1.9 multiply_reduce_fusion.9
  419.7 1.9 multiply_reduce_fusion.9
  428.5 1.9 multiply_reduce_fusion.9
  437.4 1.9 multiply_reduce_fusion.9
  446.2 1.9 multiply_reduce_fusion.9
  455.0 1.9 multiply_reduce_fusion.9
  463.8 1.9 multiply_reduce_fusion.9
  472.6 1.9 multiply_reduce_fusion.9
  481.5 1.9 multiply_reduce_fusion.9
  490.3 1.9 multiply_reduce_fusion.9
  499.1 1.9 multiply_reduce_fusion.9
  507.9 1.9 multiply_reduce_fusion.9
  516.8 1.9 multiply_reduce_fusion.9
  525.6 1.9 multiply_reduce_fusion.9
  534.4 1.9 multiply_reduce_fusion.9
  587.3 1.9 multiply_reduce_fusion.9
  605.0 1.9 multiply_reduce_fusion.9
  640.3 1.9 multiply_reduce_fusion.9
  737.3 1.9 multiply_reduce_fusion.9
  799.1 1.9 multiply_reduce_fusion.9
  876.5 159.7 %all-gather.1 = f32[16,3,4]{2,1,0:T(4,128)S(1)} all-gather(f32[1,3,4]{2,1,0:T(4,128)S(1)} %convolution_bitcast_fusion), channel_id=2, replica_groups=mesh['tank'=2,'slab'=4,'cross'=2,'sub'=2] {'slab','cross','sub'}, dimensions={0}, use_global_device_ids=true | all-gather | bytes 816 | tf_op jit(solution)/shard_map/all_gather | solution.py:152
  (1869 shorter events, 645.4 us)
Async XLA Ops:
  0.6 17.1 %copy-start.2 = (s32[8,16]{1,0:T(8,128)S(1)}, s32[8,16]{1,0:T(8,128)}, u32[]{:S(2)}) copy-start(s32[8,16]{1,0:T(8,128)} %param.20) | copy-start | bytes 1540
  0.6 19.9 %copy-start.1 = (f32[3,8,16,128]{3,2,1,0:T(8,128)S(1)}, f32[3,8,16,128]{3,2,1,0:T(8,128)}, u32[]{:S(2)}) copy-start(f32[3,8,16,128]{3,2,1,0:T(8,128)} %param.15) | copy-start | bytes 589828
  0.7 19.9 %copy-start = (f32[3,8,16,128]{3,2,1,0:T(8,128)S(1)}, f32[3,8,16,128]{3,2,1,0:T(8,128)}, u32[]{:S(2)}) copy-start(f32[3,8,16,128]{3,2,1,0:T(8,128)} %param.16) | copy-start | bytes 589828
  0.7 17.1 %copy-start.3 = (s32[1,1,1152]{2,1,0:T(1,128)S(1)}, s32[1,1,1152]{2,1,0:T(1,128)}, u32[]{:S(2)}) copy-start(s32[1,1,1152]{2,1,0:T(1,128)} %param.18) | copy-start | bytes 13828
  2.3 7.0 collective-permute-start
  7.3 6.1 collective-permute-start.1
  14.4 3.4 collective-permute-start.2
  15.7 4.8 collective-permute-start.3
  21.0 357.8 %copy-start.4 = (s32[8,16]{1,0:T(8,128)S(1)}, s32[8,16]{1,0:T(8,128)}, u32[]{:S(2)}) copy-start(s32[8,16]{1,0:T(8,128)} %param.21) | copy-start | bytes 1540
  288.9 2.7 collective-permute-start.4
  290.2 78.9 %collective-permute-start.5 = (f32[1,16,1,128]{3,1,2,0:T(8,128)S(1)}, f32[1,16,1,128]{3,1,2,0:T(8,128)S(1)}, u32[]{:S(2)}, u32[]{:S(2)}) collective-permute-start(f32[1,16,1,128]{3,1,2,0:T(8,128)S(1)} %get-tuple-element.279), channel_id=1, source_target_pairs={{4,0},{8,4},{12,8},{5,1},{9,5},{13,9},{6,2},{10,6},{14,10},{7,3},{... | collective-permute-start | bytes 24584 | tf_op jit(solution)/shard_map/ppermute | solution.py:23
  369.1 9.8 collective-permute-start.6
  377.3 3.7 collective-permute-start.7
